TPU v7x, 1024 devices: a whole 8x8x8 slice. The times are simulated.
1024 devices in a mesh: dp: 64 (over z, x), row: 4 (over y_hi, core), col: 4 (over y_lo).
Axes of the slice: x: 8, y: 8 (y_hi: 2, y_lo: 4; y = y_hi * 4 + y_lo), z: 8, core: 2. Of those that a mesh axis runs over, the one named last changes fastest.
Arguments:
- attn_mix: bfloat16 [98304, 8192], P(('dp', 'col'), 'row'), may hold values from -24 to 24
- value_weight: bfloat16 [8192, 1024], P('row', 'col'), may hold values from -0.0625 to 0.0625
- readout: bfloat16 [98304, 1024], P(('dp', 'row'), 'col'), may hold values from -0.0390625 to 0.0390625
- ref_scores: float32 [384, 2], replicated, may hold values from -6 to 6
- domain_label: int32 [384, 1], replicated, may hold values from 0 to 15
- prior_weights: float32 [16], replicated, may hold values from 0.01 to 0.1
Outputs:
- grad_weight: float32 [8192, 1024], P(('row', 'dp'), 'col')
- new_weights: float32 [16], replicated
Inputs may be any that keep to these rules, and one draw needn't show every extreme that they name: `domain_label`: every domain labels at least one pair.
All inputs are finite; a program needn't handle non-finite values.
Results may differ from a plain program's by a relative error of at most 0.0029.
Values may be sent and summed in bfloat16 or wider, within the bound.
A program may use at most 32 MiB of HBM per device.

v0:
```python
import jax
import jax.numpy as jnp
from jax import lax
from jax.sharding import PartitionSpec as P

DOMAINS = 16
SEQ = 128
PAIRS_GRP = 6


def local(attn_mix, value_weight, readout, ref_scores, domain_label, prior_weights):
    whole_rows = lax.all_gather(attn_mix, "col", axis=0, tiled=True)
    whole_read = lax.all_gather(readout, "row", axis=0, tiled=True)
    values = jnp.dot(whole_rows, value_weight, preferred_element_type=jnp.float32)
    per_token = jnp.sum(values * whole_read.astype(jnp.float32), axis=1)
    partial_value = per_token.reshape(PAIRS_GRP, 2, SEQ).sum(axis=2)
    group = lax.axis_index("dp")
    labels = domain_label[:, 0]
    domains = jnp.arange(DOMAINS, dtype=jnp.int32)
    onehot_all = (labels[:, None] == domains[None, :]).astype(jnp.float32)
    counts = jnp.sum(onehot_all, axis=0)
    start = group * PAIRS_GRP
    ref_group = lax.dynamic_slice_in_dim(ref_scores, start, PAIRS_GRP, 0)
    onehot_grp = lax.dynamic_slice_in_dim(onehot_all, start, PAIRS_GRP, 0)
    scores = lax.psum(partial_value, ("row", "col"))
    margin = scores[:, 0] - ref_group[:, 0] - (scores[:, 1] - ref_group[:, 1])
    pair_loss = jax.nn.softplus(-margin)
    loss_part = jnp.sum(onehot_grp * pair_loss[:, None], axis=0)
    loss_sums = lax.psum(loss_part, "dp")
    domain_loss = loss_sums / counts
    raised = prior_weights * jnp.exp(domain_loss)
    new_weights = raised / jnp.sum(raised)
    per_domain = new_weights / counts
    total_pairs = labels.shape[0]
    coeff = (
        total_pairs * jax.nn.sigmoid(-margin) * jnp.sum(onehot_grp * per_domain[None, :], axis=1)
    )
    signed = coeff[:, None] * jnp.array([-1.0, 1.0], dtype=jnp.float32)[None, :]
    tok_coef = jnp.broadcast_to(signed[:, :, None], (PAIRS_GRP, 2, SEQ)).reshape(
        whole_rows.shape[0]
    )
    token_grad = (tok_coef[:, None] * whole_read.astype(jnp.float32)).astype(jnp.bfloat16)
    grad_weight = lax.psum_scatter(
        lax.dot_general(
            whole_rows, token_grad, (((0,), (0,)), ((), ())), preferred_element_type=jnp.float32
        ),
        "dp",
        scatter_dimension=0,
        tiled=True,
    )
    return (grad_weight, new_weights)


def solution(mesh):
    placed = (P(("dp", "col"), "row"), P("row", "col"), P(("dp", "row"), "col"), P(), P(), P())
    return jax.shard_map(
        local, mesh=mesh, in_specs=placed, out_specs=(P(("row", "dp"), "col"), P()), check_vma=False
    )
```

profile of v0, /device:TPU:14, one launch (start us, length us, event | category | flops | bytes accessed | tf_op | source)
XLA Modules:
  0.0 581.1 jit_solution(17681727700012446566)
XLA Ops:
  7.2 0.0 copy-start
  7.2 0.0 all-gather.2.cloned.1.call-start
  7.2 0.7 all-gather.2.cloned.1.call-update
  7.9 0.0 reduce-scatter.4.cloned.1.call-start
  8.0 0.7 reduce
  8.7 0.8 constant_dynamic-slice_fusion
  9.4 0.1 copy.34
  9.5 1.1 copy.23
  10.6 15.4 %all_gather.7 = bf16[1536,256]{0,1:T(8,128)(2,1)S(1)} all-gather(bf16[384,256]{0,1:T(8,128)(2,1)S(1)} %copy.23), channel_id=1, replica_groups=mesh['dp'=64,'row'=4,'col'=4] {'row'}, dimensions={0}, use_global_device_ids=true | all-gather | bytes 983040 | tf_op jit(solution)/shard_map/all_gather | solution.py:13
  26.1 0.0 copy-start.1
  26.1 0.0 copy-start.2
  26.1 0.0 copy-start.3
  26.1 119.7 %all-gather.2.cloned.1.call-done = bf16[1536,2048]{1,0:T(8,128)(2,1)} async-done(((bf16[384,2048]{1,0:T(8,128)(2,1)}), bf16[1536,2048]{1,0:T(8,128)(2,1)}) %all-gather.2.cloned.1.call-update) | async-done | bytes 6291472 | tf_op jit(solution)/shard_map/all_gather | solution.py:12
  145.8 0.0 copy-done
  145.8 4.6 fusion.1
  150.4 0.0 copy-done.1
  150.5 0.1 reduce_sum.57
  150.5 0.1 copy.35
  150.6 27.1 %psum.14 = f32[6,2]{1,0:T(8,128)S(1)} all-reduce(f32[6,2]{1,0:T(8,128)S(1)} %reduce_sum.57), channel_id=1, replica_groups=mesh['dp'=64,'row'=4,'col'=4] {'row','col'}, use_global_device_ids=true, to_apply=%region_2.0 | all-reduce | flops 12 | bytes 96 | tf_op jit(solution)/shard_map/psum | solution.py:25
  177.7 0.2 fusion.6
  177.9 0.2 multiply_reduce_fusion.1
  178.1 0.1 fusion.5
  178.3 132.0 %psum.15 = f32[16]{0:T(128)S(1)} all-reduce(f32[16]{0:T(128)S(1)} %multiply_reduce_fusion.1), channel_id=1, replica_groups=mesh['dp'=64,'row'=4,'col'=4] {'dp'}, use_global_device_ids=true, to_apply=%region_4.5 | all-reduce | flops 16 | bytes 128 | tf_op jit(solution)/shard_map/psum | solution.py:29
  310.3 0.0 copy-done.2
  310.3 0.6 fusion.7
  310.9 1.2 broadcast_divide_fusion
  312.0 0.1 multiply_reduce_fusion
  312.1 0.1 copy.27
  312.2 0.1 multiply_reduce_fusion.2
  312.4 0.0 copy-done.3
  312.4 0.1 broadcast_multiply_fusion
  312.4 0.1 broadcast_in_dim.2
  312.5 4.8 convolution_bitcast_fusion
  317.4 1.9 copy.29
  319.2 0.0 reduce-scatter.4.cloned.1.call-update
  319.3 255.0 %reduce-scatter.4.cloned.1.call-done = f32[32,256]{1,0:T(8,128)} async-done(((f32[2048,256]{1,0:T(8,128)}), f32[32,256]{1,0:T(8,128)}) %reduce-scatter.4.cloned.1.call-update) | async-done | bytes 32784
  (4 shorter events, 0.0 us)
Async XLA Ops:
  7.2 138.6 %copy-start = (bf16[2048,256]{1,0:T(8,128)(2,1)S(1)}, bf16[2048,256]{1,0:T(8,128)(2,1)}, u32[]{:S(2)}) copy-start(bf16[2048,256]{1,0:T(8,128)(2,1)} %param.8) | copy-start | bytes 3145732
  7.2 138.6 %all-gather.2.cloned.1.call-start = ((), (), s32[]{:S(2)}) async-start(), calls=%async_computation.1 | async-start | bytes 7864320 | tf_op jit(solution)/shard_map/all_gather | solution.py:12
  7.9 566.3 %reduce-scatter.4.cloned.1.call-start = ((), (), s32[]{:S(2)}) async-start(), calls=%async_computation.2 | async-start | bytes 2129920
  26.1 124.3 %copy-start.1 = (bf16[1536,256]{0,1:T(8,128)(2,1)}, bf16[1536,256]{0,1:T(8,128)(2,1)S(1)}, u32[]{:S(2)}) copy-start(bf16[1536,256]{0,1:T(8,128)(2,1)S(1)} %all_gather.7) | copy-start | bytes 2359300
  26.1 284.2 %copy-start.2 = (f32[16]{0:T(128)S(1)}, f32[16]{0:T(128)}, u32[]{:S(2)}) copy-start(f32[16]{0:T(128)} %param.12) | copy-start | bytes 196
  26.1 286.3 %copy-start.3 = (f32[2]{0:T(128)S(1)}, f32[2]{0:T(128)}, u32[]{:S(2)}) copy-start(f32[2]{0:T(128)} %constant.22.clone) | copy-start | bytes 28
Sparse Core Ops, SparseCore 0:
  10.7 135.0 all-gather.1
  319.4 254.8 reduce-scatter.3
where the time goes:
time: 582 us; the launch traced here: 581 us
  waiting for transfers between devices  375 us (64%)
  blocking collectives  175 us (30%)
  between operations  14.1 us (2%)
  matrix products  9.46 us (2%)
    unnamed x3, waiting for transfers between devices  256 us
    psum x1, blocking collectives, local(): loss_sums = lax.psum(loss_part, 'dp')  132 us
    all_gather x1, waiting for transfers between devices, local(): whole_rows = lax.all_gather(attn_mix, 'col', axis=0, tiled=True)  120 us
    psum x1, blocking collectives, local(): scores = lax.psum(partial_value, ('row', 'col'))  27.1 us
    all_gather x1, blocking collectives, local(): whole_read = lax.all_gather(readout, 'row', axis=0, tiled=True)  15.4 us
  transfers between devices with their start and end apart: 2, of which 2 were waited for; matrix products, arithmetic and copies ran while one was open for 0% of the time, Pallas kernels for 0%

commit v1 on v0

v1 whole, which is shorter than its diff:
```python
import functools

import jax
import jax.numpy as jnp
from jax import lax
from jax.experimental import pallas as pl
from jax.experimental.pallas import tpu as pltpu
from jax.sharding import PartitionSpec as P

DOMAINS = 16
SEQ = 128
PARTS = 4
MESH = pl.DeviceIdType.MESH


def kernel(
    nz, nx, nr, nc,
    x_ref, w_ref, r_ref, ref_ref, label_ref, prior_ref,
    grad_ref, weights_ref,
    wbuf, rbuf, xt, tg, line, rowx, rowz, stage, got, send2, got2, sum3, got3,
    wy_s, wy_r, w1_s, w1_r, w2_s, w2_r, r_s, r_r,
    l_s, l_r, x_s, x_r, z_s, z_r, p1_s, p1_r, p2_s, p2_r, p3_s, p3_r,
):
    tb, feat = x_ref.shape
    ob = w_ref.shape[1]
    fb = feat // (nz * nx)
    sb = nc * ob // PARTS
    resp = tb // SEQ
    pairs_grp = nc * resp // 2
    all_pairs = label_ref.shape[1]
    per_col = ob // sb
    f32 = jnp.float32

    dp, row, col = lax.axis_index("dp"), lax.axis_index("row"), lax.axis_index("col")
    z, x = dp // nx, dp % nx
    me = row * nc + col
    nline = nr * nc

    def at_line(k):
        idx = lax.rem(me + k, nline)
        return (dp, idx // nc, idx % nc)

    def at_x(k):
        return (z * nx + lax.rem(x + k, nx), row, col)

    def at_z(k):
        return (lax.rem(z + k, nz) * nx + x, row, col)

    def at_col(k):
        return (dp, row, lax.rem(col + k, nc))

    def send(src, dst, ssem, rsem, dev):
        copy = pltpu.make_async_remote_copy(
            src_ref=src, dst_ref=dst, send_sem=ssem, recv_sem=rsem,
            device_id=dev, device_id_type=MESH,
        )
        copy.start()
        return copy

    sent = []
    axes = ((x, nx, at_x), (z, nz, at_z))

    barrier = pltpu.get_barrier_semaphore()
    for k in range(1, nline):
        pl.semaphore_signal(barrier, inc=1, device_id=at_line(k), device_id_type=MESH)
    for _, n, at in axes:
        for k in range(1, n):
            pl.semaphore_signal(barrier, inc=1, device_id=at(k), device_id_type=MESH)
    pl.semaphore_wait(barrier, nline - 1 + nx - 1 + nz - 1)

    rows = pl.ds(pl.multiple_of(dp * fb, fb), fb)
    wy = []
    for k in range(1, nc):
        slot = nc - k - 1
        wy.append(send(w_ref.at[rows, :], wbuf.at[slot, z, x], wy_s.at[k], wy_r.at[slot], at_col(k)))

    reads = []
    for k in range(1, nr):
        reads.append(send(r_ref, rbuf.at[col], r_s.at[k], r_r.at[col], (dp, lax.rem(row + k, nr), row)))
    own_read = pltpu.make_async_copy(r_ref, rbuf.at[col], r_r.at[col])
    far_read = pltpu.make_async_remote_copy(
        src_ref=r_ref, dst_ref=rbuf.at[col], send_sem=r_s.at[0], recv_sem=r_r.at[col],
        device_id=(dp, row, row), device_id_type=MESH,
    )

    @pl.when(row == col)
    def _():
        own_read.start()

    @pl.when(row != col)
    def _():
        far_read.start()

    lanes = (pl.ds(0, ob // 2), pl.ds(ob // 2, ob // 2))
    w1 = [[], []]
    if nc > 1:
        for slot in range(nc - 1):
            pltpu.make_async_copy(wbuf.at[slot, z, x], wbuf.at[slot, z, x], wy_r.at[slot]).wait()
        for k in range(1, max(nx, nz)):
            for h, (_, n, at) in enumerate(axes):
                if k < n:
                    block = wbuf.at[:, z, x, :, lanes[h]]
                    w1[h].append(send(block, block, w1_s.at[h, k], w1_r.at[h, k], at(k)))

    for b in range(nz):
        block = x_ref[:, b * nx * fb:(b + 1) * nx * fb]
        xt[b] = jnp.swapaxes(block, 0, 1).reshape(nx, fb, tb)
    lane = lax.broadcasted_iota(jnp.int32, (1, all_pairs), 1)
    onehot = (label_ref[...] == lax.broadcasted_iota(jnp.int32, (DOMAINS, all_pairs), 0)).astype(f32)
    counts = jnp.sum(onehot, axis=1, keepdims=True)

    if nc > 1:
        for h in range(2):
            for copy in w1[h]:
                copy.wait_recv()
        chains = []
        for h in range(2):
            pos, n, at = axes[1 - h]
            for d, (sign, length) in enumerate(((1, n // 2), (-1, n - 1 - n // 2))):
                for slot in range(nc - 1):
                    chains.append((h, d, slot, pos, n, at, sign, length))
        moving = {}
        for s in range(max(nx, nz) // 2 + 1):
            for h, d, slot, pos, n, at, sign, length in chains:
                if 0 < s <= length:
                    moving[h, d, slot, s - 1].wait_recv()
                if s < length:
                    src = lax.rem(pos - sign * s + n, n)
                    if h == 0:
                        block = wbuf.at[slot, src, :, :, lanes[h]]
                    else:
                        block = wbuf.at[slot, :, src, :, lanes[h]]
                    moving[h, d, slot, s] = send(
                        block, block, w2_s.at[h, d, slot, s], w2_r.at[h, d, slot, s], at(sign % n)
                    )
        sent += wy + w1[0] + w1[1] + list(moving.values())

    for j in range(nc):
        pltpu.make_async_copy(rbuf.at[j], rbuf.at[j], r_r.at[j]).wait()
    sums = [jnp.zeros((1, ob), f32) for _ in range(resp)]
    for k in range(nc):
        weight = w_ref[...] if k == 0 else wbuf[k - 1].reshape(feat, ob)
        values = jnp.dot(x_ref[...], weight, preferred_element_type=f32)
        prod = values * rbuf[lax.rem(col + k, nc)].astype(f32)
        for q in range(resp):
            sums[q] = sums[q] + jnp.sum(prod[q * SEQ:(q + 1) * SEQ], axis=0, keepdims=True)
    mine = jnp.zeros((1, all_pairs), f32)
    for q in range(resp):
        which = col * resp + q
        score = jnp.sum(sums[q], axis=1, keepdims=True)
        sign = jnp.where(which % 2 == 0, 1.0, -1.0).astype(f32)
        mine = mine + jnp.where(lane == dp * pairs_grp + which // 2, sign * score, 0.0)

    def exchange(buf, pos, n, at, ssem, rsem, value):
        buf[pos] = value
        copies = [send(buf.at[pos], buf.at[pos], ssem.at[k], rsem.at[k], at(k)) for k in range(1, n)]
        for copy in copies:
            copy.wait_recv()
        total = buf[0]
        for i in range(1, n):
            total = total + buf[i]
        sent.extend(copies)
        return total

    mine = exchange(line, me, nline, at_line, l_s, l_r, mine)
    mine = exchange(rowx, x, nx, at_x, x_s, x_r, mine)
    mine = exchange(rowz, z, nz, at_z, z_s, z_r, mine)
    margin = mine - (ref_ref[0:1, :] - ref_ref[1:2, :])
    loss = jnp.maximum(-margin, 0.0) + jnp.log1p(jnp.exp(-jnp.abs(margin)))
    domain_loss = jnp.sum(onehot * loss, axis=1, keepdims=True) / counts
    eye = lax.broadcasted_iota(jnp.int32, (DOMAINS, DOMAINS), 0) == lax.broadcasted_iota(
        jnp.int32, (DOMAINS, DOMAINS), 1
    )
    prior = jnp.sum(jnp.where(eye, prior_ref[...], 0.0), axis=1, keepdims=True)
    raised = prior * jnp.exp(domain_loss)
    new_weights = raised / jnp.sum(raised, axis=0, keepdims=True)
    weights_ref[...] = jnp.sum(jnp.where(eye, new_weights, 0.0), axis=0, keepdims=True)
    coeff = (
        all_pairs * jax.nn.sigmoid(-margin)
        * jnp.sum(onehot * (new_weights / counts), axis=0, keepdims=True)
    )
    for q in range(resp):
        which = col * resp + q
        own = jnp.sum(
            jnp.where(lane == dp * pairs_grp + which // 2, coeff, 0.0), axis=1, keepdims=True
        )
        own = own * jnp.where(which % 2 == 0, -1.0, 1.0).astype(f32)
        for j in range(PARTS):
            at_lane = (j % per_col) * sb
            block = rbuf[j // per_col, q * SEQ:(q + 1) * SEQ, at_lane:at_lane + sb]
            tg[j, q * SEQ:(q + 1) * SEQ, :] = (own * block.astype(f32)).astype(jnp.bfloat16)

    def part(h, target, j):
        lhs = xt[:, target] if h == 0 else xt[target]
        lhs = lhs.reshape(lhs.shape[0] * fb, tb)
        return jnp.dot(lhs, tg[2 * h + j], preferred_element_type=f32)

    chains = []
    for h in range(2):
        pos, n, at = axes[h]
        for j in range(2):
            long = n // 2
            lengths = (long, n - 1 - long) if j == 0 else (n - 1 - long, long)
            for d in range(2):
                chains.append((h, d, j, pos, n, at, 1 - 2 * d, lengths[d]))
    moving = {}
    for s in range(max(nx, nz) // 2):
        for h, d, j, pos, n, at, sign, length in chains:
            if s < length:
                chunk = part(h, lax.rem(pos + sign * (length - s) + n, n), j)
                if s > 0:
                    moving[h, d, j, s - 1].wait_recv()
                    chunk = chunk + got[h, d, j, s - 1].astype(f32)
                stage[h, d, j, s] = chunk.astype(jnp.bfloat16)
                moving[h, d, j, s] = send(
                    stage.at[h, d, j, s], got.at[h, d, j, s],
                    p1_s.at[h, d, j, s], p1_r.at[h, d, j, s], at(sign % n),
                )
    for h in range(2):
        pos, n, at = axes[h]
        for j in range(2):
            chunk = part(h, pos, j)
            for ch in chains:
                if ch[0] == h and ch[2] == j and ch[7] > 0:
                    last = ch[7] - 1
                    moving[h, ch[1], j, last].wait_recv()
                    chunk = chunk + got[h, ch[1], j, last].astype(f32)
            send2[h, :, j] = chunk.reshape(chunk.shape[0] // fb, fb, sb)
    sent += list(moving.values())

    second = []
    for h in range(2):
        pos, n, at = axes[1 - h]
        for k in range(1, n):
            second.append(send(
                send2.at[h, lax.rem(pos + k, n)], got2.at[h, pos], p2_s.at[h, k], p2_r.at[h, k], at(k)
            ))
    for copy in second:
        copy.wait_recv()
    sent += second
    for h in range(2):
        pos, n, at = axes[1 - h]
        total = send2[h, pos]
        for k in range(1, n):
            total = total + got2[h, lax.rem(pos - k + n, n)]
        sum3[2 * h:2 * h + 2] = total

    third = []
    for k in range(1, nc):
        target = lax.rem(col + k, nc)
        third.append(send(
            sum3.at[pl.ds(target * per_col, per_col)], got3.at[col], p3_s.at[k], p3_r.at[k], at_col(k)
        ))
    for copy in third:
        copy.wait_recv()
    sent += third
    for i in range(per_col):
        total = sum3[col * per_col + i]
        for k in range(1, nc):
            total = total + got3[lax.rem(col - k + nc, nc), i]
        grad_ref[:, i * sb:(i + 1) * sb] = total

    for copy in reads + sent:
        copy.wait_send()

    @pl.when(row != col)
    def _():
        far_read.wait_send()


def local(nz, nx, nr, nc, attn_mix, value_weight, readout, ref_scores, domain_label, prior_weights):
    tb, feat = attn_mix.shape
    ob = value_weight.shape[1]
    fb = feat // (nz * nx)
    sb = nc * ob // PARTS
    all_pairs = domain_label.shape[0]
    ring = max(nz, nx)
    vmem = pl.BlockSpec(memory_space=pltpu.VMEM)
    bf16, f32 = jnp.bfloat16, jnp.float32
    dma = pltpu.SemaphoreType.DMA
    assert nz == nx
    grad, weights = pl.pallas_call(
        functools.partial(kernel, nz, nx, nr, nc),
        out_shape=(
            jax.ShapeDtypeStruct((fb, ob), f32),
            jax.ShapeDtypeStruct((1, DOMAINS), f32),
        ),
        in_specs=[vmem] * 6,
        out_specs=(vmem, vmem),
        scratch_shapes=[
            pltpu.VMEM((max(nc - 1, 1), nz, nx, fb, ob), bf16),
            pltpu.VMEM((nc, tb, ob), bf16),
            pltpu.VMEM((nz, nx, fb, tb), bf16),
            pltpu.VMEM((PARTS, tb, sb), bf16),
            pltpu.VMEM((nr * nc, 1, all_pairs), f32),
            pltpu.VMEM((nx, 1, all_pairs), f32),
            pltpu.VMEM((nz, 1, all_pairs), f32),
            pltpu.VMEM((2, 2, 2, ring // 2, ring * fb, sb), bf16),
            pltpu.VMEM((2, 2, 2, ring // 2, ring * fb, sb), bf16),
            pltpu.VMEM((2, ring, 2, fb, sb), f32),
            pltpu.VMEM((2, ring, 2, fb, sb), f32),
            pltpu.VMEM((PARTS, fb, sb), f32),
            pltpu.VMEM((nc, ob // sb, fb, sb), f32),
            dma((nc,)), dma((nc,)),
            dma((2, ring)), dma((2, ring)),
            dma((2, 2, max(nc - 1, 1), ring // 2)), dma((2, 2, max(nc - 1, 1), ring // 2)),
            dma((nr,)), dma((nc,)),
            dma((nr * nc,)), dma((nr * nc,)),
            dma((nx,)), dma((nx,)),
            dma((nz,)), dma((nz,)),
            dma((2, 2, 2, ring // 2)), dma((2, 2, 2, ring // 2)),
            dma((2, ring)), dma((2, ring)),
            dma((nc,)), dma((nc,)),
        ],
        compiler_params=pltpu.CompilerParams(
            collective_id=0, has_side_effects=True, vmem_limit_bytes=48 * 1024 * 1024
        ),
        cost_estimate=pl.CostEstimate(
            flops=4 * tb * feat * nc * ob, bytes_accessed=4 * tb * feat, transcendentals=0
        ),
    )(attn_mix, value_weight, readout, ref_scores.T, domain_label.T, prior_weights.reshape(1, DOMAINS))
    return grad, weights.reshape(DOMAINS)


def build(mesh, nz, nx):
    placed = (P(("dp", "col"), "row"), P("row", "col"), P(("dp", "row"), "col"), P(), P(), P())
    return jax.shard_map(
        functools.partial(local, nz, nx, mesh.shape["row"], mesh.shape["col"]),
        mesh=mesh, in_specs=placed, out_specs=(P(("row", "dp"), "col"), P()), check_vma=False,
    )


def solution(mesh):
    return build(mesh, 8, mesh.shape["dp"] // 8)
```

time: 582 us -> 134 us (0.23)
  waiting for transfers between devices: 375 us -> 0 us
  blocking collectives: 175 us -> 0 us
  Pallas kernels: 0 us -> 125 us
  between operations: 14.1 us -> 0.65 us
  matrix products: 9.46 us -> 0 us
    unnamed x3 -> x0, waiting for transfers between devices: 256 us -> none
    psum x2 -> x0, blocking collectives: 159 us -> none  [the longest x1 132 us: local(): loss_sums = lax.psum(loss_part, 'dp')]
    pallas_call x0 -> x1, Pallas kernels: none -> 125 us  [local(): pl.pallas_call(functools.partial(kernel, nz, nx, nr, nc), out_shape=(jax....]
    all_gather x1 -> x0, waiting for transfers between devices: 120 us -> none  [local(): whole_rows = lax.all_gather(attn_mix, 'col', axis=0, tiled=True)]
    all_gather x1 -> x0, blocking collectives: 15.4 us -> none  [local(): whole_read = lax.all_gather(readout, 'row', axis=0, tiled=True)]
    dot_general x2 -> x0, matrix products: 9.46 us -> none  [the longest x1 4.83 us: local(): lax.dot_general(whole_rows, token_grad, (((0,), (0,)), ((), ())), preferr...]
  transfers between devices with their start and end apart: 2 -> 0, of which waited for: 2 -> 0; matrix products, arithmetic and copies ran while one was open for 0% -> 0% of each run, Pallas kernels for 0% -> 0%
where the time goes in v1:
time: 134 us; the launch traced here: 132 us
  Pallas kernels  125 us (93%)
  local copies, waits for them, and re-layouts  6.7 us (5%)
    pallas_call x1, Pallas kernels, local(): pl.pallas_call(functools.partial(kernel, nz, nx, nr, nc), out_shape=(jax....  125 us
    unnamed x14, local copies, waits for them, and re-layouts  6.7 us

profile of v1, /device:TPU:14, one launch (start us, length us, event | category | flops | bytes accessed | tf_op | source)
XLA Modules:
  0.0 132.4 jit_solution(1072380384628891489)
XLA Ops:
  0.6 0.0 copy-start
  0.6 1.4 %copy-done = bf16[384,2048]{1,0:T(8,128)(2,1)S(1)} copy-done((bf16[384,2048]{1,0:T(8,128)(2,1)S(1)}, bf16[384,2048]{1,0:T(8,128)(2,1)}, u32[]{:S(2)}) %copy-start) | copy-done | bytes 1572888
  2.0 0.0 copy-start.1
  2.0 1.2 copy-done.1
  3.3 0.0 copy-start.2
  3.3 0.9 copy-done.2
  4.2 0.0 copy-start.3
  4.2 0.7 copy-done.3
  4.9 0.0 copy-start.4
  4.9 0.7 copy-done.4
  5.6 0.0 copy-start.5
  5.6 0.7 copy-done.5
  6.2 125.1 %shard_map.77 = (f32[32,256]{1,0:T(8,128)S(1)}, f32[1,16]{1,0:T(1,128)S(1)}) custom-call(bf16[384,2048]{1,0:T(8,128)(2,1)S(1)} %copy-done, bf16[2048,256]{1,0:T(8,128)(2,1)S(1)} %copy-done.1, bf16[384,256]{1,0:T(8,128)(2,1)S(1)} %copy-done.2, f32[2,384]{1,0:T(2,128)S(1)} %bitcast.4, s32[1,384]{1,0:T(1,128)S(1)} %bitcast.5, f32[1,16]{1,0:T(1,128)S(1)} %bitcast.6), custom_call_target="tpu_custom_call" | custom-call | flops 3221225472 | bytes 3145728 | tf_op jit(solution)/shard_map/pallas_call | solution.py:282
  131.3 0.6 copy.10
  131.9 0.5 copy.11
Async XLA Ops:
  0.6 1.4 %copy-start = (bf16[384,2048]{1,0:T(8,128)(2,1)S(1)}, bf16[384,2048]{1,0:T(8,128)(2,1)}, u32[]{:S(2)}) copy-start(bf16[384,2048]{1,0:T(8,128)(2,1)} %x_ref.1) | copy-start | bytes 4718596
  2.0 1.2 copy-start.1
  3.3 0.9 copy-start.2
  4.2 0.7 copy-start.3
  4.9 0.7 copy-start.4
  5.6 0.7 copy-start.5

commit v2 on v1

v2 whole, which is shorter than its diff:
```python
import functools

import jax
import jax.numpy as jnp
from jax import lax
from jax.experimental import pallas as pl
from jax.experimental.pallas import tpu as pltpu
from jax.sharding import PartitionSpec as P

DOMAINS = 16
SEQ = 128
PARTS = 4
CUTS = 2
FAR = 3
MESH = pl.DeviceIdType.MESH


def kernel(
    nz, nx, nr, nc,
    x_hbm, w_hbm, r_hbm, ref_hbm, label_hbm, prior_hbm,
    grad_ref, weights_ref,
    x_ref, w_ref, r_ref, ref_ref, label_ref, prior_ref,
    wbuf, rbuf, xt, tg, rowc, rowy, rowx, rowz, stage, got, send2, got2, far2, gotfar2, sum3, got3,
    in_s, wy_s, wy_r, w2_s, w2_r, r_s, r_r, f_s,
    c_s, c_r, y_s, y_r, x_s, x_r, z_s, z_r, p1_s, p1_r, p2_s, p2_r, p3_s, p3_r,
):
    tb, feat = x_ref.shape
    ob = w_ref.shape[-1]
    fb = feat // (nz * nx)
    sb = nc * ob // PARTS
    resp = tb // SEQ
    pairs_grp = nc * resp // 2
    all_pairs = label_ref.shape[1]
    per_col = ob // sb
    f32 = jnp.float32

    dp, row, col = lax.axis_index("dp"), lax.axis_index("row"), lax.axis_index("col")
    z, x = dp // nx, dp % nx
    cores = 2 if nr % 2 == 0 else 1
    y_high, core = row // cores, row % cores
    y, ny = y_high * nc + col, nr // cores * nc

    def at_core(k):
        return (dp, y_high * cores + lax.rem(core + k, cores), col)

    def at_y(k):
        other = lax.rem(y + k, ny)
        return (dp, other // nc * cores + core, other % nc)

    def at_x(k):
        return (z * nx + lax.rem(x + k, nx), row, col)

    def at_z(k):
        return (lax.rem(z + k, nz) * nx + x, row, col)

    def at_col(k):
        return (dp, row, lax.rem(col + k, nc))

    def send(src, dst, ssem, rsem, dev):
        copy = pltpu.make_async_remote_copy(
            src_ref=src, dst_ref=dst, send_sem=ssem, recv_sem=rsem,
            device_id=dev, device_id_type=MESH,
        )
        copy.start()
        return copy

    sent = []
    axes = ((x, nx, at_x), (z, nz, at_z))

    loads = []
    for i, (src, dst) in enumerate((
        (w_hbm, w_ref), (r_hbm, r_ref), (x_hbm, x_ref),
        (label_hbm, label_ref), (ref_hbm, ref_ref), (prior_hbm, prior_ref),
    )):
        loads.append(pltpu.make_async_copy(src, dst, in_s.at[i]))
        loads[i].start()

    barrier = pltpu.get_barrier_semaphore()
    count = 0
    for n, at in ((cores, at_core), (ny, at_y), (nx, at_x), (nz, at_z)):
        for k in range(1, n):
            pl.semaphore_signal(barrier, inc=1, device_id=at(k), device_id_type=MESH)
            count += 1
    loads[0].wait()
    loads[1].wait()
    pl.semaphore_wait(barrier, count)

    lanes = (pl.ds(0, ob // 2), pl.ds(ob // 2, ob // 2))

    def w_block(ref, h, i):
        return ref.at[i, :, :, lanes[h]] if h == 0 else ref.at[:, i, :, lanes[h]]

    wy = []
    for k in range(1, nc):
        slot = nc - k - 1
        for h, i in enumerate((z, x)):
            wy.append(send(
                w_block(w_ref, h, i), w_block(wbuf.at[slot], h, i),
                wy_s.at[h, k], wy_r.at[h, slot], at_col(k),
            ))

    reads = []
    for k in range(1, nr // cores):
        there = lax.rem(y_high + k, nr // cores) * cores + core
        reads.append(send(r_ref, rbuf.at[col], r_s.at[k], r_r.at[col], (dp, there, row)))
    own_read = pltpu.make_async_copy(r_ref, rbuf.at[col], r_r.at[col])
    far_read = pltpu.make_async_remote_copy(
        src_ref=r_ref, dst_ref=rbuf.at[col], send_sem=r_s.at[0], recv_sem=r_r.at[col],
        device_id=(dp, row, row), device_id_type=MESH,
    )

    @pl.when(row == col)
    def _():
        own_read.start()

    @pl.when(row != col)
    def _():
        far_read.start()

    for load in loads[2:]:
        load.wait()
    for b in range(nz):
        block = x_ref[:, b * nx * fb:(b + 1) * nx * fb]
        xt[b] = jnp.swapaxes(block, 0, 1).reshape(nx, fb, tb)
    lane = lax.broadcasted_iota(jnp.int32, (1, all_pairs), 1)
    onehot = (label_ref[...] == lax.broadcasted_iota(jnp.int32, (DOMAINS, all_pairs), 0)).astype(f32)
    counts = jnp.sum(onehot, axis=1, keepdims=True)

    chains, moving = [], {}
    for slot in range(nc - 1):
        for h in range(2):
            pos, n, at = axes[1 - h]
            for d, sign in enumerate((1, -1)):
                length = n // 2 if (h + slot + d) % 2 == 0 else n - 1 - n // 2
                chains.append((h, d, slot, pos, n, at, sign, length))

    def spread(s):
        for h, d, slot, pos, n, at, sign, length in chains:
            if s == 0 and d == 0:
                block = w_block(wbuf.at[slot], h, pos)
                pltpu.make_async_copy(block, block, wy_r.at[h, slot]).wait()
            if 0 < s <= length:
                moving[h, d, slot, s - 1].wait_recv()
            if s < length:
                block = w_block(wbuf.at[slot], h, lax.rem(pos - sign * s + n, n))
                moving[h, d, slot, s] = send(
                    block, block, w2_s.at[h, d, slot, s], w2_r.at[h, d, slot, s], at(sign % n)
                )

    spread(0)

    passes = [
        pltpu.make_async_remote_copy(
            src_ref=rbuf.at[j], dst_ref=rbuf.at[j], send_sem=f_s.at[j], recv_sem=r_r.at[j],
            device_id=at_core(1), device_id_type=MESH,
        )
        for j in range(nc if cores > 1 else 0)
    ]
    passing = core == col % cores

    def pass_on():
        for j in range(nc):
            pltpu.make_async_copy(rbuf.at[j], rbuf.at[j], r_r.at[j]).wait()
            if cores > 1:
                @pl.when(passing)
                def _():
                    passes[j].start()

    steps = max(nx, nz) // 2
    for s in range(1, steps):
        spread(s)
    pass_on()
    spread(steps)
    sent += wy + list(moving.values())

    sums = [jnp.zeros((1, ob), f32) for _ in range(resp)]
    for k in range(nc):
        weight = (w_ref[...] if k == 0 else wbuf[k - 1]).reshape(feat, ob)
        values = jnp.dot(x_ref[...], weight, preferred_element_type=f32)
        prod = values * rbuf[lax.rem(col + k, nc)].astype(f32)
        for q in range(resp):
            sums[q] = sums[q] + jnp.sum(prod[q * SEQ:(q + 1) * SEQ], axis=0, keepdims=True)
    mine = jnp.zeros((1, all_pairs), f32)
    for q in range(resp):
        which = col * resp + q
        score = jnp.sum(sums[q], axis=1, keepdims=True)
        sign = jnp.where(which % 2 == 0, 1.0, -1.0).astype(f32)
        mine = mine + jnp.where(lane == dp * pairs_grp + which // 2, sign * score, 0.0)

    def exchange(buf, pos, n, at, ssem, rsem, value):
        buf[pos] = value
        copies = [send(buf.at[pos], buf.at[pos], ssem.at[k], rsem.at[k], at(k)) for k in range(1, n)]
        for copy in copies:
            copy.wait_recv()
        total = buf[0]
        for i in range(1, n):
            total = total + buf[i]
        sent.extend(copies)
        return total

    mine = exchange(rowc, core, cores, at_core, c_s, c_r, mine)
    mine = exchange(rowy, y, ny, at_y, y_s, y_r, mine)
    mine = exchange(rowx, x, nx, at_x, x_s, x_r, mine)
    mine = exchange(rowz, z, nz, at_z, z_s, z_r, mine)
    margin = mine - (ref_ref[0:1, :] - ref_ref[1:2, :])
    loss = jnp.maximum(-margin, 0.0) + jnp.log1p(jnp.exp(-jnp.abs(margin)))
    domain_loss = jnp.sum(onehot * loss, axis=1, keepdims=True) / counts
    eye = lax.broadcasted_iota(jnp.int32, (DOMAINS, DOMAINS), 0) == lax.broadcasted_iota(
        jnp.int32, (DOMAINS, DOMAINS), 1
    )
    prior = jnp.sum(jnp.where(eye, prior_ref[...], 0.0), axis=1, keepdims=True)
    raised = prior * jnp.exp(domain_loss)
    new_weights = raised / jnp.sum(raised, axis=0, keepdims=True)
    weights_ref[...] = jnp.sum(jnp.where(eye, new_weights, 0.0), axis=0, keepdims=True)
    coeff = (
        all_pairs * jax.nn.sigmoid(-margin)
        * jnp.sum(onehot * (new_weights / counts), axis=0, keepdims=True)
    )
    for q in range(resp):
        which = col * resp + q
        own = jnp.sum(
            jnp.where(lane == dp * pairs_grp + which // 2, coeff, 0.0), axis=1, keepdims=True
        )
        own = own * jnp.where(which % 2 == 0, -1.0, 1.0).astype(f32)
        for j in range(PARTS):
            at_lane = (j % per_col) * sb
            block = rbuf[j // per_col, q * SEQ:(q + 1) * SEQ, at_lane:at_lane + sb]
            tg[j, q * SEQ:(q + 1) * SEQ, :] = (own * block.astype(f32)).astype(jnp.bfloat16)

    def part(h, target, j):
        lhs = xt[:, target] if h == 0 else xt[target]
        lhs = lhs.reshape(lhs.shape[0] * fb, tb)
        return jnp.dot(lhs, tg[2 * h + j], preferred_element_type=f32)

    chains = []
    for j in range(2):
        for h in range(2):
            pos, n, at = axes[h]
            long = n // 2
            lengths = (long, n - 1 - long) if j == 0 else (n - 1 - long, long)
            for d in range(2):
                chains.append((h, d, j, pos, n, at, 1 - 2 * d, lengths[d]))
    moving = {}
    for s in range(max(nx, nz) // 2):
        for h, d, j, pos, n, at, sign, length in chains:
            if s < length:
                chunk = part(h, lax.rem(pos + sign * (length - s) + n, n), j)
                for u in range(CUTS):
                    piece = chunk[u * n * fb // CUTS:(u + 1) * n * fb // CUTS]
                    if s > 0:
                        moving[h, d, j, s - 1, u].wait_recv()
                        piece = piece + got[h, d, j, s - 1, u].astype(f32)
                    stage[h, d, j, s, u] = piece.astype(jnp.bfloat16)
                    moving[h, d, j, s, u] = send(
                        stage.at[h, d, j, s, u], got.at[h, d, j, s, u],
                        p1_s.at[h, d, j, s, u], p1_r.at[h, d, j, s, u], at(sign % n),
                    )
    for h in range(2):
        pos, n, at = axes[h]
        for j in range(2):
            chunk = part(h, pos, j)
            for ch in chains:
                if ch[0] == h and ch[2] == j and ch[7] > 0:
                    last = ch[7] - 1
                    for u in range(CUTS):
                        moving[h, ch[1], j, last, u].wait_recv()
                    chunk = chunk + got[h, ch[1], j, last].reshape(n * fb, sb).astype(f32)
            send2[h, :, j] = chunk.reshape(chunk.shape[0] // fb, fb, sb)
    sent += list(moving.values())

    second = []
    for h in range(2):
        pos, n, at = axes[1 - h]
        for k in sorted(range(1, n), key=lambda k: -min(k, n - k)):
            target, src, dst = lax.rem(pos + k, n), send2, got2
            if min(k, n - k) >= FAR:
                far2[h, target] = send2[h, target].astype(jnp.bfloat16)
                src, dst = far2, gotfar2
            second.append(send(
                src.at[h, target], dst.at[h, pos], p2_s.at[h, k], p2_r.at[h, k], at(k)
            ))
    for copy in second:
        copy.wait_recv()
    sent += second
    for h in range(2):
        pos, n, at = axes[1 - h]
        total = send2[h, pos]
        for k in range(1, n):
            there = gotfar2 if min(k, n - k) >= FAR else got2
            total = total + there[h, lax.rem(pos - k + n, n)].astype(f32)
        sum3[2 * h:2 * h + 2] = total

    third = []
    for k in range(1, nc):
        target = lax.rem(col + k, nc)
        third.append(send(
            sum3.at[pl.ds(target * per_col, per_col)], got3.at[col], p3_s.at[k], p3_r.at[k], at_col(k)
        ))
    for copy in third:
        copy.wait_recv()
    sent += third
    for i in range(per_col):
        total = sum3[col * per_col + i]
        for k in range(1, nc):
            total = total + got3[lax.rem(col - k + nc, nc), i]
        grad_ref[:, i * sb:(i + 1) * sb] = total

    for copy in reads + sent:
        copy.wait_send()

    @pl.when(row != col)
    def _():
        far_read.wait_send()

    if cores > 1:
        @pl.when(passing)
        def _():
            for copy in passes:
                copy.wait_send()


def local(nz, nx, nr, nc, attn_mix, value_weight, readout, ref_scores, domain_label, prior_weights):
    tb, feat = attn_mix.shape
    ob = value_weight.shape[1]
    fb = feat // (nz * nx)
    sb = nc * ob // PARTS
    all_pairs = domain_label.shape[0]
    ring = max(nz, nx)
    cores = 2 if nr % 2 == 0 else 1
    ny = nr // cores * nc
    vmem = pl.BlockSpec(memory_space=pltpu.VMEM)
    bf16, f32 = jnp.bfloat16, jnp.float32
    dma = pltpu.SemaphoreType.DMA
    assert nz == nx
    grad, weights = pl.pallas_call(
        functools.partial(kernel, nz, nx, nr, nc),
        out_shape=(
            jax.ShapeDtypeStruct((fb, ob), f32),
            jax.ShapeDtypeStruct((1, DOMAINS), f32),
        ),
        in_specs=[pl.BlockSpec(memory_space=pl.ANY)] * 6,
        out_specs=(vmem, vmem),
        scratch_shapes=[
            pltpu.VMEM(attn_mix.shape, bf16),
            pltpu.VMEM((nz, nx, fb, ob), bf16),
            pltpu.VMEM(readout.shape, bf16),
            pltpu.VMEM((2, all_pairs), f32),
            pltpu.VMEM((1, all_pairs), jnp.int32),
            pltpu.VMEM((1, DOMAINS), f32),
            pltpu.VMEM((max(nc - 1, 1), nz, nx, fb, ob), bf16),
            pltpu.VMEM((nc, tb, ob), bf16),
            pltpu.VMEM((nz, nx, fb, tb), bf16),
            pltpu.VMEM((PARTS, tb, sb), bf16),
            pltpu.VMEM((cores, 1, all_pairs), f32),
            pltpu.VMEM((ny, 1, all_pairs), f32),
            pltpu.VMEM((nx, 1, all_pairs), f32),
            pltpu.VMEM((nz, 1, all_pairs), f32),
            pltpu.VMEM((2, 2, 2, ring // 2, CUTS, ring * fb // CUTS, sb), bf16),
            pltpu.VMEM((2, 2, 2, ring // 2, CUTS, ring * fb // CUTS, sb), bf16),
            pltpu.VMEM((2, ring, 2, fb, sb), f32),
            pltpu.VMEM((2, ring, 2, fb, sb), f32),
            pltpu.VMEM((2, ring, 2, fb, sb), bf16),
            pltpu.VMEM((2, ring, 2, fb, sb), bf16),
            pltpu.VMEM((PARTS, fb, sb), f32),
            pltpu.VMEM((nc, ob // sb, fb, sb), f32),
            dma((6,)),
            dma((2, nc)), dma((2, nc)),
            dma((2, 2, max(nc - 1, 1), ring // 2)), dma((2, 2, max(nc - 1, 1), ring // 2)),
            dma((nr,)), dma((nc,)), dma((nc,)),
            dma((cores,)), dma((cores,)),
            dma((ny,)), dma((ny,)),
            dma((nx,)), dma((nx,)),
            dma((nz,)), dma((nz,)),
            dma((2, 2, 2, ring // 2, CUTS)), dma((2, 2, 2, ring // 2, CUTS)),
            dma((2, ring)), dma((2, ring)),
            dma((nc,)), dma((nc,)),
        ],
        compiler_params=pltpu.CompilerParams(
            collective_id=0, has_side_effects=True, vmem_limit_bytes=56 * 1024 * 1024
        ),
        cost_estimate=pl.CostEstimate(
            flops=4 * tb * feat * nc * ob, bytes_accessed=4 * tb * feat, transcendentals=0
        ),
    )(
        attn_mix, value_weight.reshape(nz, nx, fb, ob), readout,
        ref_scores.T, domain_label.T, prior_weights.reshape(1, DOMAINS),
    )
    return grad, weights.reshape(DOMAINS)


def build(mesh, nz, nx):
    placed = (P(("dp", "col"), "row"), P("row", "col"), P(("dp", "row"), "col"), P(), P(), P())
    return jax.shard_map(
        functools.partial(local, nz, nx, mesh.shape["row"], mesh.shape["col"]),
        mesh=mesh, in_specs=placed, out_specs=(P(("row", "dp"), "col"), P()), check_vma=False,
    )


def solution(mesh):
    return build(mesh, 8, mesh.shape["dp"] // 8)
```

time: 134 us -> 120 us (0.90); the launches traced: 132 us -> 120 us
  Pallas kernels: 125 us -> 117 us
  local copies, waits for them, and re-layouts: 6.7 us -> 2.55 us
    pallas_call x1, Pallas kernels: 125 us -> 117 us  [local(): pl.pallas_call(functools.partial(kernel, nz, nx, nr, nc), out_shape=(jax....]
    unnamed x14 -> x2, local copies, waits for them, and re-layouts: 6.7 us -> 2.55 us
where the time goes in v2:
time: 120 us
  Pallas kernels  117 us (98%)
  local copies, waits for them, and re-layouts  2.55 us (2%)
    pallas_call x1, Pallas kernels, local(): pl.pallas_call(functools.partial(kernel, nz, nx, nr, nc), out_shape=(jax....  117 us
    unnamed x2, local copies, waits for them, and re-layouts  2.55 us

profile of v2, /device:TPU:14, one launch (start us, length us, event | category | flops | bytes accessed | tf_op | source)
XLA Modules:
  0.0 119.8 jit_solution(14339231681442445651)
XLA Ops:
  0.6 116.6 %shard_map.77 = (f32[32,256]{1,0:T(8,128)}, f32[1,16]{1,0:T(1,128)}) custom-call(bf16[384,2048]{1,0:T(8,128)(2,1)} %x_hbm.1, bf16[8,8,32,256]{3,2,1,0:T(8,128)(2,1)} %bitcast.5, bf16[384,256]{1,0:T(8,128)(2,1)} %r_hbm.1, f32[2,384]{1,0:T(2,128)} %bitcast.6, s32[1,384]{1,0:T(1,128)} %bitcast.7, f32[1,16]{1,0:T(1,128)} %bitcast.8), custom_call_target="tpu_custom_call" | custom-call | flops 3221225472 | bytes 3145728 | tf_op jit(solution)/shard_map/pallas_call | solution.py:335
  117.2 1.4 %copy.10 = f32[32,256]{1,0:T(8,128)} copy(f32[32,256]{1,0:T(8,128)} %get-tuple-element.8) | data formatting | bytes 65536
  118.6 1.2 copy.11

commit v3 on v2

--- a/solution.py
+++ b/solution.py
@@ -10,7 +10,6 @@
 DOMAINS = 16
 SEQ = 128
 PARTS = 4
-CUTS = 2
 FAR = 3
 MESH = pl.DeviceIdType.MESH
 
@@ -21,13 +20,17 @@
     grad_ref, weights_ref,
     x_ref, w_ref, r_ref, ref_ref, label_ref, prior_ref,
     wbuf, rbuf, xt, tg, rowc, rowy, rowx, rowz, stage, got, send2, got2, far2, gotfar2, sum3, got3,
+    xtp, rp, tgp, sump, gotp,
     in_s, wy_s, wy_r, w2_s, w2_r, r_s, r_r, f_s,
     c_s, c_r, y_s, y_r, x_s, x_r, z_s, z_r, p1_s, p1_r, p2_s, p2_r, p3_s, p3_r,
+    pair_s, pair_r,
 ):
     tb, feat = x_ref.shape
     ob = w_ref.shape[-1]
     fb = feat // (nz * nx)
+    hb = fb // 2
     sb = nc * ob // PARTS
+    paired = nc == PARTS
     resp = tb // SEQ
     pairs_grp = nc * resp // 2
     all_pairs = label_ref.shape[1]
@@ -55,6 +58,9 @@
 
     def at_col(k):
         return (dp, row, lax.rem(col + k, nc))
+
+    odd = col % 2
+    pair = (dp, row, col + 1 - 2 * odd)
 
     def send(src, dst, ssem, rsem, dev):
         copy = pltpu.make_async_remote_copy(
@@ -121,7 +127,9 @@
         load.wait()
     for b in range(nz):
         block = x_ref[:, b * nx * fb:(b + 1) * nx * fb]
-        xt[b] = jnp.swapaxes(block, 0, 1).reshape(nx, fb, tb)
+        block = jnp.swapaxes(block, 0, 1).reshape(nx, 2, hb, tb)
+        xt[0, b] = block[:, 0]
+        xt[1, b] = block[:, 1]
     lane = lax.broadcasted_iota(jnp.int32, (1, all_pairs), 1)
     onehot = (label_ref[...] == lax.broadcasted_iota(jnp.int32, (DOMAINS, all_pairs), 0)).astype(f32)
     counts = jnp.sum(onehot, axis=1, keepdims=True)
@@ -147,6 +155,8 @@
                     block, block, w2_s.at[h, d, slot, s], w2_r.at[h, d, slot, s], at(sign % n)
                 )
 
+    if paired:
+        sent.append(send(xt.at[0], xtp, pair_s.at[2], pair_r.at[2], pair))
     spread(0)
 
     passes = [
@@ -167,10 +177,20 @@
                     passes[j].start()
 
     steps = max(nx, nz) // 2
+    def readout_ready():
+        pass_on()
+        if paired:
+            for h in range(2):
+                sent.append(send(rbuf.at[2 * h + 1 - odd], rp.at[h], pair_s.at[h], pair_r.at[h], pair))
+
     for s in range(1, steps):
+        if s == max(steps - 1, 1):
+            readout_ready()
         spread(s)
-    pass_on()
-    spread(steps)
+    if steps < 2:
+        readout_ready()
+    if steps > 0:
+        spread(steps)
     sent += wy + list(moving.values())
 
     sums = [jnp.zeros((1, ob), f32) for _ in range(resp)]
@@ -216,56 +236,79 @@
         all_pairs * jax.nn.sigmoid(-margin)
         * jnp.sum(onehot * (new_weights / counts), axis=0, keepdims=True)
     )
-    for q in range(resp):
-        which = col * resp + q
+    def scaled(column, q, block):
+        which = column * resp + q
         own = jnp.sum(
             jnp.where(lane == dp * pairs_grp + which // 2, coeff, 0.0), axis=1, keepdims=True
         )
         own = own * jnp.where(which % 2 == 0, -1.0, 1.0).astype(f32)
+        return (own * block.astype(f32)).astype(jnp.bfloat16)
+
+    for q in range(resp):
+        tokens = slice(q * SEQ, (q + 1) * SEQ)
         for j in range(PARTS):
             at_lane = (j % per_col) * sb
-            block = rbuf[j // per_col, q * SEQ:(q + 1) * SEQ, at_lane:at_lane + sb]
-            tg[j, q * SEQ:(q + 1) * SEQ, :] = (own * block.astype(f32)).astype(jnp.bfloat16)
-
-    def part(h, target, j):
-        lhs = xt[:, target] if h == 0 else xt[target]
-        lhs = lhs.reshape(lhs.shape[0] * fb, tb)
-        return jnp.dot(lhs, tg[2 * h + j], preferred_element_type=f32)
+            tg[j, tokens, :] = scaled(col, q, rbuf[j // per_col, tokens, at_lane:at_lane + sb])
+
+    def pair_ready():
+        for i in range(3):
+            there = rp.at[i] if i < 2 else xtp
+            pltpu.make_async_copy(there, there, pair_r.at[i]).wait()
+        for q in range(resp):
+            tokens = slice(q * SEQ, (q + 1) * SEQ)
+            for h in range(2):
+                tgp[h, tokens, :] = scaled(pair[2], q, rp[h, tokens, :])
+
+    if paired:
+        units = ((1, 0, False), (1, 1, False), (0, 0, True))
+    else:
+        units = tuple((half, j, False) for half in range(2) for j in range(2))
+
+    def part(h, target, unit):
+        half, j, both = unit
+        lhs = xt[half, :, target] if h == 0 else xt[half, target]
+        lhs = lhs.reshape(lhs.shape[0] * hb, tb)
+        if not both:
+            return jnp.dot(lhs, tg[2 * h + j], preferred_element_type=f32)
+        far = xtp[:, target] if h == 0 else xtp[target]
+        return jnp.dot(lhs, tg[2 * h + odd], preferred_element_type=f32) + jnp.dot(
+            far.reshape(lhs.shape), tgp[h], preferred_element_type=f32
+        )
 
     chains = []
-    for j in range(2):
+    for u in range(len(units)):
         for h in range(2):
             pos, n, at = axes[h]
-            long = n // 2
-            lengths = (long, n - 1 - long) if j == 0 else (n - 1 - long, long)
             for d in range(2):
-                chains.append((h, d, j, pos, n, at, 1 - 2 * d, lengths[d]))
+                length = n // 2 if (u + h + d) % 2 == 0 else n - 1 - n // 2
+                chains.append((h, d, u, pos, n, at, 1 - 2 * d, length))
     moving = {}
-    for s in range(max(nx, nz) // 2):
-        for h, d, j, pos, n, at, sign, length in chains:
+    if paired and steps < 1:
+        pair_ready()
+    for s in range(steps):
+        for h, d, u, pos, n, at, sign, length in chains:
             if s < length:
-                chunk = part(h, lax.rem(pos + sign * (length - s) + n, n), j)
-                for u in range(CUTS):
-                    piece = chunk[u * n * fb // CUTS:(u + 1) * n * fb // CUTS]
-                    if s > 0:
-                        moving[h, d, j, s - 1, u].wait_recv()
-                        piece = piece + got[h, d, j, s - 1, u].astype(f32)
-                    stage[h, d, j, s, u] = piece.astype(jnp.bfloat16)
-                    moving[h, d, j, s, u] = send(
-                        stage.at[h, d, j, s, u], got.at[h, d, j, s, u],
-                        p1_s.at[h, d, j, s, u], p1_r.at[h, d, j, s, u], at(sign % n),
-                    )
-    for h in range(2):
-        pos, n, at = axes[h]
-        for j in range(2):
-            chunk = part(h, pos, j)
+                if s == 0 and units[u][2] and (h, d) == (0, 0):
+                    pair_ready()
+                chunk = part(h, lax.rem(pos + sign * (length - s) + n, n), units[u])
+                if s > 0:
+                    moving[h, d, u, s - 1].wait_recv()
+                    chunk = chunk + got[h, d, u, s - 1].astype(f32)
+                stage[h, d, u, s] = chunk.astype(jnp.bfloat16)
+                moving[h, d, u, s] = send(
+                    stage.at[h, d, u, s], got.at[h, d, u, s],
+                    p1_s.at[h, d, u, s], p1_r.at[h, d, u, s], at(sign % n),
+                )
+    for u in range(len(units)):
+        for h in range(2):
+            pos, n, at = axes[h]
+            chunk = part(h, pos, units[u])
             for ch in chains:
-                if ch[0] == h and ch[2] == j and ch[7] > 0:
+                if ch[0] == h and ch[2] == u and ch[7] > 0:
                     last = ch[7] - 1
-                    for u in range(CUTS):
-                        moving[h, ch[1], j, last, u].wait_recv()
-                    chunk = chunk + got[h, ch[1], j, last].reshape(n * fb, sb).astype(f32)
-            send2[h, :, j] = chunk.reshape(chunk.shape[0] // fb, fb, sb)
+                    moving[h, ch[1], u, last].wait_recv()
+                    chunk = chunk + got[h, ch[1], u, last].astype(f32)
+            send2[h, :, u] = chunk.reshape(n, hb, sb)
     sent += list(moving.values())
 
     second = []
@@ -288,7 +331,11 @@
         for k in range(1, n):
             there = gotfar2 if min(k, n - k) >= FAR else got2
             total = total + there[h, lax.rem(pos - k + n, n)].astype(f32)
-        sum3[2 * h:2 * h + 2] = total
+        for u, (half, j, both) in enumerate(units):
+            if both:
+                sump[h] = total[u]
+            else:
+                sum3[2 * h + j, 0 if paired else half] = total[u]
 
     third = []
     for k in range(1, nc):
@@ -296,6 +343,8 @@
         third.append(send(
             sum3.at[pl.ds(target * per_col, per_col)], got3.at[col], p3_s.at[k], p3_r.at[k], at_col(k)
         ))
+    if paired:
+        third.append(send(sump.at[1 - col // 2], gotp, pair_s.at[3], pair_r.at[3], at_col(2)))
     for copy in third:
         copy.wait_recv()
     sent += third
@@ -303,7 +352,12 @@
         total = sum3[col * per_col + i]
         for k in range(1, nc):
             total = total + got3[lax.rem(col - k + nc, nc), i]
-        grad_ref[:, i * sb:(i + 1) * sb] = total
+        at_lane = slice(i * sb, (i + 1) * sb)
+        if paired:
+            grad_ref[hb:, at_lane] = total[0]
+            grad_ref[:hb, at_lane] = sump[col // 2] + gotp[...]
+        else:
+            grad_ref[:, at_lane] = total.reshape(fb, sb)
 
     for copy in reads + sent:
         copy.wait_send()
@@ -326,6 +380,9 @@
     sb = nc * ob // PARTS
     all_pairs = domain_label.shape[0]
     ring = max(nz, nx)
+    hb = fb // 2
+    paired = nc == PARTS
+    units = 3 if paired else 4
     cores = 2 if nr % 2 == 0 else 1
     ny = nr // cores * nc
     vmem = pl.BlockSpec(memory_space=pltpu.VMEM)
@@ -349,31 +406,37 @@
             pltpu.VMEM((1, DOMAINS), f32),
             pltpu.VMEM((max(nc - 1, 1), nz, nx, fb, ob), bf16),
             pltpu.VMEM((nc, tb, ob), bf16),
-            pltpu.VMEM((nz, nx, fb, tb), bf16),
+            pltpu.VMEM((2, nz, nx, hb, tb), bf16),
             pltpu.VMEM((PARTS, tb, sb), bf16),
             pltpu.VMEM((cores, 1, all_pairs), f32),
             pltpu.VMEM((ny, 1, all_pairs), f32),
             pltpu.VMEM((nx, 1, all_pairs), f32),
             pltpu.VMEM((nz, 1, all_pairs), f32),
-            pltpu.VMEM((2, 2, 2, ring // 2, CUTS, ring * fb // CUTS, sb), bf16),
-            pltpu.VMEM((2, 2, 2, ring // 2, CUTS, ring * fb // CUTS, sb), bf16),
-            pltpu.VMEM((2, ring, 2, fb, sb), f32),
-            pltpu.VMEM((2, ring, 2, fb, sb), f32),
-            pltpu.VMEM((2, ring, 2, fb, sb), bf16),
-            pltpu.VMEM((2, ring, 2, fb, sb), bf16),
-            pltpu.VMEM((PARTS, fb, sb), f32),
-            pltpu.VMEM((nc, ob // sb, fb, sb), f32),
+            pltpu.VMEM((2, 2, 4, max(ring // 2, 1), ring * hb, sb), bf16),
+            pltpu.VMEM((2, 2, 4, max(ring // 2, 1), ring * hb, sb), bf16),
+            pltpu.VMEM((2, ring, units, hb, sb), f32),
+            pltpu.VMEM((2, ring, units, hb, sb), f32),
+            pltpu.VMEM((2, ring, units, hb, sb), bf16),
+            pltpu.VMEM((2, ring, units, hb, sb), bf16),
+            pltpu.VMEM((PARTS, 1 if paired else 2, hb, sb), f32),
+            pltpu.VMEM((nc, ob // sb, 1 if paired else 2, hb, sb), f32),
+            pltpu.VMEM((nz, nx, hb, tb), bf16),
+            pltpu.VMEM((2, tb, sb), bf16),
+            pltpu.VMEM((2, tb, sb), bf16),
+            pltpu.VMEM((2, hb, sb), f32),
+            pltpu.VMEM((hb, sb), f32),
             dma((6,)),
             dma((2, nc)), dma((2, nc)),
-            dma((2, 2, max(nc - 1, 1), ring // 2)), dma((2, 2, max(nc - 1, 1), ring // 2)),
+            dma((2, 2, max(nc - 1, 1), max(ring // 2, 1))), dma((2, 2, max(nc - 1, 1), max(ring // 2, 1))),
             dma((nr,)), dma((nc,)), dma((nc,)),
             dma((cores,)), dma((cores,)),
             dma((ny,)), dma((ny,)),
             dma((nx,)), dma((nx,)),
             dma((nz,)), dma((nz,)),
-            dma((2, 2, 2, ring // 2, CUTS)), dma((2, 2, 2, ring // 2, CUTS)),
+            dma((2, 2, 4, max(ring // 2, 1))), dma((2, 2, 4, max(ring // 2, 1))),
             dma((2, ring)), dma((2, ring)),
             dma((nc,)), dma((nc,)),
+            dma((4,)), dma((4,)),
         ],
         compiler_params=pltpu.CompilerParams(
             collective_id=0, has_side_effects=True, vmem_limit_bytes=56 * 1024 * 1024

time: 120 us -> 116 us (0.967)
  Pallas kernels: 117 us -> 112 us
    pallas_call x1, Pallas kernels: 117 us -> 112 us  [local(): pl.pallas_call(functools.partial(kernel, nz, nx, nr, nc), out_shape=(jax....]
where the time goes in v3:
time: 116 us; the launch traced here: 115 us
  Pallas kernels  112 us (97%)
  local copies, waits for them, and re-layouts  2.55 us (2%)
    pallas_call x1, Pallas kernels, local(): pl.pallas_call(functools.partial(kernel, nz, nx, nr, nc), out_shape=(jax....  112 us
    unnamed x2, local copies, waits for them, and re-layouts  2.55 us

profile of v3, /device:TPU:14, one launch (start us, length us, event | category | flops | bytes accessed | tf_op | source)
XLA Modules:
  0.0 115.2 jit_solution(957041565136595473)
XLA Ops:
  0.6 112.0 %shard_map.77 = (f32[32,256]{1,0:T(8,128)}, f32[1,16]{1,0:T(1,128)}) custom-call(bf16[384,2048]{1,0:T(8,128)(2,1)} %x_hbm.1, bf16[8,8,32,256]{3,2,1,0:T(8,128)(2,1)} %bitcast.5, bf16[384,256]{1,0:T(8,128)(2,1)} %r_hbm.1, f32[2,384]{1,0:T(2,128)} %bitcast.6, s32[1,384]{1,0:T(1,128)} %bitcast.7, f32[1,16]{1,0:T(1,128)} %bitcast.8), custom_call_target="tpu_custom_call" | custom-call | flops 3221225472 | bytes 3145728 | tf_op jit(solution)/shard_map/pallas_call | solution.py:392
  112.6 1.4 %copy.10 = f32[32,256]{1,0:T(8,128)} copy(f32[32,256]{1,0:T(8,128)} %get-tuple-element.8) | data formatting | bytes 65536
  114.0 1.2 %copy.11 = f32[16]{0:T(128)} copy(f32[16]{0:T(128)} %bitcast.9) | data formatting | bytes 128

commit v4 on v3

--- a/solution.py
+++ b/solution.py
@@ -177,6 +177,13 @@
                     passes[j].start()
 
     steps = max(nx, nz) // 2
+    def add_scores(k):
+        weight = (w_ref[...] if k == 0 else wbuf[k - 1]).reshape(feat, ob)
+        values = jnp.dot(x_ref[...], weight, preferred_element_type=f32)
+        prod = values * rbuf[lax.rem(col + k, nc)].astype(f32)
+        for q in range(resp):
+            sums[q] = sums[q] + jnp.sum(prod[q * SEQ:(q + 1) * SEQ], axis=0, keepdims=True)
+
     def readout_ready():
         pass_on()
         if paired:
@@ -189,17 +196,14 @@
         spread(s)
     if steps < 2:
         readout_ready()
+    sums = [jnp.zeros((1, ob), f32) for _ in range(resp)]
+    add_scores(0)
     if steps > 0:
         spread(steps)
     sent += wy + list(moving.values())
 
-    sums = [jnp.zeros((1, ob), f32) for _ in range(resp)]
-    for k in range(nc):
-        weight = (w_ref[...] if k == 0 else wbuf[k - 1]).reshape(feat, ob)
-        values = jnp.dot(x_ref[...], weight, preferred_element_type=f32)
-        prod = values * rbuf[lax.rem(col + k, nc)].astype(f32)
-        for q in range(resp):
-            sums[q] = sums[q] + jnp.sum(prod[q * SEQ:(q + 1) * SEQ], axis=0, keepdims=True)
+    for k in range(1, nc):
+        add_scores(k)
     mine = jnp.zeros((1, all_pairs), f32)
     for q in range(resp):
         which = col * resp + q
@@ -299,20 +303,9 @@
                     stage.at[h, d, u, s], got.at[h, d, u, s],
                     p1_s.at[h, d, u, s], p1_r.at[h, d, u, s], at(sign % n),
                 )
-    for u in range(len(units)):
-        for h in range(2):
-            pos, n, at = axes[h]
-            chunk = part(h, pos, units[u])
-            for ch in chains:
-                if ch[0] == h and ch[2] == u and ch[7] > 0:
-                    last = ch[7] - 1
-                    moving[h, ch[1], u, last].wait_recv()
-                    chunk = chunk + got[h, ch[1], u, last].astype(f32)
-            send2[h, :, u] = chunk.reshape(n, hb, sb)
-    sent += list(moving.values())
-
     second = []
-    for h in range(2):
+
+    def second_phase(h):
         pos, n, at = axes[1 - h]
         for k in sorted(range(1, n), key=lambda k: -min(k, n - k)):
             target, src, dst = lax.rem(pos + k, n), send2, got2
@@ -322,6 +315,20 @@
             second.append(send(
                 src.at[h, target], dst.at[h, pos], p2_s.at[h, k], p2_r.at[h, k], at(k)
             ))
+
+    for h in range(2):
+        pos, n, at = axes[h]
+        for u in range(len(units)):
+            chunk = part(h, pos, units[u])
+            for ch in chains:
+                if ch[0] == h and ch[2] == u and ch[7] > 0:
+                    last = ch[7] - 1
+                    moving[h, ch[1], u, last].wait_recv()
+                    chunk = chunk + got[h, ch[1], u, last].astype(f32)
+            send2[h, :, u] = chunk.reshape(n, hb, sb)
+        second_phase(h)
+    sent += list(moving.values())
+
     for copy in second:
         copy.wait_recv()
     sent += second

time: 116 us -> 116 us (level)
  no operation moved by 1% of the time
where the time goes in v4:
time: 116 us; the launch traced here: 115 us
  Pallas kernels  112 us (97%)
  local copies, waits for them, and re-layouts  2.55 us (2%)
    pallas_call x1, Pallas kernels, local(): pl.pallas_call(functools.partial(kernel, nz, nx, nr, nc), out_shape=(jax....  112 us
    unnamed x2, local copies, waits for them, and re-layouts  2.55 us

profile of v4, /device:TPU:14, one launch (start us, length us, event | category | flops | bytes accessed | tf_op | source)
XLA Modules:
  0.0 115.0 jit_solution(11409132274989360756)
XLA Ops:
  0.6 111.8 %shard_map.77 = (f32[32,256]{1,0:T(8,128)}, f32[1,16]{1,0:T(1,128)}) custom-call(bf16[384,2048]{1,0:T(8,128)(2,1)} %x_hbm.1, bf16[8,8,32,256]{3,2,1,0:T(8,128)(2,1)} %bitcast.5, bf16[384,256]{1,0:T(8,128)(2,1)} %r_hbm.1, f32[2,384]{1,0:T(2,128)} %bitcast.6, s32[1,384]{1,0:T(1,128)} %bitcast.7, f32[1,16]{1,0:T(1,128)} %bitcast.8), custom_call_target="tpu_custom_call" | custom-call | flops 3221225472 | bytes 3145728 | tf_op jit(solution)/shard_map/pallas_call | solution.py:399
  112.4 1.4 %copy.10 = f32[32,256]{1,0:T(8,128)} copy(f32[32,256]{1,0:T(8,128)} %get-tuple-element.8) | data formatting | bytes 65536
  113.8 1.2 %copy.11 = f32[16]{0:T(128)} copy(f32[16]{0:T(128)} %bitcast.9) | data formatting | bytes 128
